TPU v7x, 512 devices: a whole 4x4x16 slice. The times are simulated.
512 devices in a mesh: gx: 32 (over x_lo, z), gy: 16 (over y, x_hi, core).
Axes of the slice: x: 4 (x_hi: 2, x_lo: 2; x = x_hi * 2 + x_lo), y: 4, z: 16, core: 2. Of those that a mesh axis runs over, the one named last changes fastest.
Arguments:
- impedance: bfloat16 [32, 16, 1024, 1024], P('gx', 'gy'), may hold values from -0.1875 to 0.1875
- rebuild_map: bfloat16 [32, 16, 256, 1024], P('gx', 'gy'), may hold values from -0.1875 to 0.1875
- left_trace: bfloat16 [32, 16, 512, 512], P('gx', 'gy'), may hold values from -6 to 6
- lower_trace: bfloat16 [32, 16, 512, 512], P('gx', 'gy'), may hold values from -6 to 6
- cell_kind: int32 [512, 256], P('gx', 'gy'), may hold values from 0 to 15
- kind_wavenum: float32 [16], replicated, may hold values from 0.5 to 3
Outputs:
- right_trace: bfloat16 [32, 16, 512, 512], P('gx', 'gy')
- upper_trace: bfloat16 [32, 16, 512, 512], P('gx', 'gy')
- residual: float32 [512, 256, 512], P('gx', 'gy')
All inputs are finite; a program needn't handle non-finite values.
Results may differ from a plain program's by a relative error of at most 0.0064.
Values may be sent and summed in bfloat16 or wider, within the bound.
A program may use at most 64 MiB of HBM per device.

v0:
```python
import jax
import jax.numpy as jnp
from jax import lax
from jax.sharding import PartitionSpec as P

STEPS = 4


def from_behind(block, axis, distance):
    devices = range(lax.axis_size(axis))
    route = [(i - distance, i) for i in devices if i - distance in devices]
    return lax.ppermute(block, axis, route)


def extended(cells, sides, width):
    for axis, dim in sides:
        count = lax.axis_size(axis)
        ends = count - 1
        head = lax.slice_in_dim(cells, 0, width, axis=dim)
        tail = lax.slice_in_dim(cells, cells.shape[dim] - width, cells.shape[dim], axis=dim)
        cells = jnp.concatenate(
            [
                lax.ppermute(tail, axis, [(i, (i + 1) % count) for i in range(ends)]),
                cells,
                lax.ppermute(head, axis, [((i + 1) % count, i) for i in range(ends)]),
            ],
            axis=dim,
        )
    return cells


def advance(mapping, left_in, lower_in):
    stacked = jnp.concatenate([left_in, lower_in], axis=0)
    outgoing = jnp.dot(mapping, stacked, preferred_element_type=jnp.float32).astype(jnp.bfloat16)
    rows = left_in.shape[0]
    return (outgoing[:rows], outgoing[rows:])


def per_device(impedance, rebuild_map, left_trace, lower_trace, cell_kind, kind_wavenum):
    mapping = impedance[0, 0]
    left_in = left_trace[0, 0]
    lower_in = lower_trace[0, 0]
    right_out, upper_out = (left_in, lower_in)
    for sweep_step in range(STEPS):
        last_turn = sweep_step + 1 == STEPS
        right_out, upper_out = advance(mapping, left_in, lower_in)
        if not last_turn:
            left_in = from_behind(right_out, "gx", 1)
            lower_in = from_behind(upper_out, "gy", 1)
    cells_x = cell_kind.shape[0]
    cells_y = cell_kind.shape[1]
    sources = left_in.shape[1]
    stacked = jnp.concatenate([left_in, lower_in], axis=0)
    volume = jnp.dot(rebuild_map[0, 0], stacked, preferred_element_type=jnp.float32).reshape(
        cells_x, cells_y, sources
    )
    padded = extended(volume.astype(jnp.bfloat16), (("gx", 0), ("gy", 1)), 1).astype(volume.dtype)
    beside = padded[2:, 1:-1] + padded[:-2, 1:-1] + padded[1:-1, 2:] + padded[1:-1, :-2]
    kind_ids = jnp.arange(kind_wavenum.shape[0], dtype=jnp.int32)
    wavenum = jnp.sum(
        jnp.where(
            cell_kind[:, :, None] == kind_ids[None, None, :],
            kind_wavenum[None, None, :],
            jnp.float32(0.0),
        ),
        axis=-1,
    )
    residual = beside - 4.0 * volume + wavenum[:, :, None] * volume
    return (right_out[None, None], upper_out[None, None], residual)


def solution(mesh):
    return jax.shard_map(
        per_device,
        mesh=mesh,
        in_specs=(
            P("gx", "gy", None, None),
            P("gx", "gy", None, None),
            P("gx", "gy", None, None),
            P("gx", "gy", None, None),
            P("gx", "gy"),
            P(),
        ),
        out_specs=(P("gx", "gy", None, None), P("gx", "gy", None, None), P("gx", "gy", None)),
        check_vma=False,
    )
```

profile of v0, /device:TPU:24, one launch (start us, length us, event | category | flops | bytes accessed | tf_op | source)
XLA Modules:
  0.0 94.8 jit_solution(18382298321234257417)
XLA Ops:
  0.6 1.6 %copy-done = bf16[1,1,1024,1024]{3,2,1,0:T(8,128)(2,1)S(1)} copy-done((bf16[1,1,1024,1024]{3,2,1,0:T(8,128)(2,1)S(1)}, bf16[1,1,1024,1024]{3,2,1,0:T(8,128)(2,1)}, u32[]{:S(2)}) %copy-start) | copy-done | bytes 2097176
  2.2 2.5 %fusion.29 = bf16[1024,512]{0,1:T(8,128)(2,1)S(1)} fusion(bf16[1,1,1024,1024]{3,2,1,0:T(8,128)(2,1)S(1)} %copy-done, bf16[512,512]{1,0:T(8,128)(2,1)} %bitcast.49, bf16[512,512]{1,0:T(8,128)(2,1)} %bitcast.50), kind=kOutput, calls=%fused_computation.15 | convolution fusion | flops 1076363264 | bytes 4194304 | tf_op jit(solution)/shard_map/dot_general | solution.py:34
  4.8 3.9 %collective-permute-start = (bf16[512,512]{0,1:T(8,128)(2,1)S(1)}, bf16[512,512]{0,1:T(8,128)(2,1)S(1)}, u32[]{:S(2)}, u32[]{:S(2)}) collective-permute-start(bf16[512,512]{0,1:T(8,128)(2,1)S(1)} %get-tuple-element.15), channel_id=1, source_target_pairs={{0,16},{16,32},{32,48},{48,64},{64,80},{80,96},{96,112},{112,128},... | collective-permute-start | bytes 1572872 | tf_op jit(solution)/shard_map/ppermute | solution.py:12
  8.7 1.9 %collective-permute-start.1 = (bf16[512,512]{0,1:T(8,128)(2,1)S(1)}, bf16[512,512]{0,1:T(8,128)(2,1)S(1)}, u32[]{:S(2)}, u32[]{:S(2)}) collective-permute-start(bf16[512,512]{0,1:T(8,128)(2,1)S(1)} %get-tuple-element.16), channel_id=1, source_target_pairs={{0,1},{1,2},{2,3},{3,4},{4,5},{5,6},{6,7},{7,8},{8,9},{9,10},{10,1... | collective-permute-start | bytes 1572872 | tf_op jit(solution)/shard_map/ppermute | solution.py:12
  10.6 9.2 %collective-permute-done = bf16[512,512]{0,1:T(8,128)(2,1)S(1)} collective-permute-done((bf16[512,512]{0,1:T(8,128)(2,1)S(1)}, bf16[512,512]{0,1:T(8,128)(2,1)S(1)}, u32[]{:S(2)}, u32[]{:S(2)}) %collective-permute-start) | collective-permute-done | bytes 524320 | tf_op jit(solution)/shard_map/ppermute | solution.py:12
  19.8 13.0 %collective-permute-done.1 = bf16[512,512]{0,1:T(8,128)(2,1)S(1)} collective-permute-done((bf16[512,512]{0,1:T(8,128)(2,1)S(1)}, bf16[512,512]{0,1:T(8,128)(2,1)S(1)}, u32[]{:S(2)}, u32[]{:S(2)}) %collective-permute-start.1) | collective-permute-done | bytes 524320 | tf_op jit(solution)/shard_map/ppermute | solution.py:12
  32.8 1.3 %fusion.26 = bf16[1024,512]{0,1:T(8,128)(2,1)S(1)} fusion(bf16[1,1,1024,1024]{3,2,1,0:T(8,128)(2,1)S(1)} %copy-done, bf16[512,512]{0,1:T(8,128)(2,1)S(1)} %collective-permute-done.1, bf16[512,512]{0,1:T(8,128)(2,1)S(1)} %collective-permute-done), kind=kOutput, calls=%fused_computation.14 | convolution fusion | flops 1076363264 | bytes 4194304 | tf_op jit(solution)/shard_map/dot_general | solution.py:34
  34.2 1.3 %collective-permute-start.2 = (bf16[512,512]{0,1:T(8,128)(2,1)S(1)}, bf16[512,512]{0,1:T(8,128)(2,1)S(1)}, u32[]{:S(2)}, u32[]{:S(2)}) collective-permute-start(bf16[512,512]{0,1:T(8,128)(2,1)S(1)} %get-tuple-element.13), channel_id=1, source_target_pairs={{0,16},{16,32},{32,48},{48,64},{64,80},{80,96},{96,112},{112,128},... | collective-permute-start | bytes 1572872 | tf_op jit(solution)/shard_map/ppermute | solution.py:12
  35.5 1.9 %collective-permute-start.3 = (bf16[512,512]{0,1:T(8,128)(2,1)S(1)}, bf16[512,512]{0,1:T(8,128)(2,1)S(1)}, u32[]{:S(2)}, u32[]{:S(2)}) collective-permute-start(bf16[512,512]{0,1:T(8,128)(2,1)S(1)} %get-tuple-element.14), channel_id=1, source_target_pairs={{0,1},{1,2},{2,3},{3,4},{4,5},{5,6},{6,7},{7,8},{8,9},{9,10},{10,1... | collective-permute-start | bytes 1572872 | tf_op jit(solution)/shard_map/ppermute | solution.py:12
  37.4 7.9 %collective-permute-done.2 = bf16[512,512]{0,1:T(8,128)(2,1)S(1)} collective-permute-done((bf16[512,512]{0,1:T(8,128)(2,1)S(1)}, bf16[512,512]{0,1:T(8,128)(2,1)S(1)}, u32[]{:S(2)}, u32[]{:S(2)}) %collective-permute-start.2) | collective-permute-done | bytes 524320 | tf_op jit(solution)/shard_map/ppermute | solution.py:12
  45.4 9.6 %collective-permute-done.3 = bf16[512,512]{0,1:T(8,128)(2,1)S(1)} collective-permute-done((bf16[512,512]{0,1:T(8,128)(2,1)S(1)}, bf16[512,512]{0,1:T(8,128)(2,1)S(1)}, u32[]{:S(2)}, u32[]{:S(2)}) %collective-permute-start.3) | collective-permute-done | bytes 524320 | tf_op jit(solution)/shard_map/ppermute | solution.py:12
  54.9 1.3 %fusion.23 = bf16[1024,512]{0,1:T(8,128)(2,1)S(1)} fusion(bf16[1,1,1024,1024]{3,2,1,0:T(8,128)(2,1)S(1)} %copy-done, bf16[512,512]{0,1:T(8,128)(2,1)S(1)} %collective-permute-done.3, bf16[512,512]{0,1:T(8,128)(2,1)S(1)} %collective-permute-done.2), kind=kOutput, calls=%fused_computation.13 | convolution fusion | flops 1076363264 | bytes 4194304 | tf_op jit(solution)/shard_map/dot_general | solution.py:34
  56.3 1.5 %collective-permute-start.4 = (bf16[512,512]{0,1:T(8,128)(2,1)S(1)}, bf16[512,512]{0,1:T(8,128)(2,1)S(1)}, u32[]{:S(2)}, u32[]{:S(2)}) collective-permute-start(bf16[512,512]{0,1:T(8,128)(2,1)S(1)} %get-tuple-element.12), channel_id=1, source_target_pairs={{0,16},{16,32},{32,48},{48,64},{64,80},{80,96},{96,112},{112,128},... | collective-permute-start | bytes 1572872 | tf_op jit(solution)/shard_map/ppermute | solution.py:12
  57.8 1.9 %collective-permute-start.5 = (bf16[512,512]{0,1:T(8,128)(2,1)S(1)}, bf16[512,512]{0,1:T(8,128)(2,1)S(1)}, u32[]{:S(2)}, u32[]{:S(2)}) collective-permute-start(bf16[512,512]{0,1:T(8,128)(2,1)S(1)} %get-tuple-element.11), channel_id=1, source_target_pairs={{0,1},{1,2},{2,3},{3,4},{4,5},{5,6},{6,7},{7,8},{8,9},{9,10},{10,1... | collective-permute-start | bytes 1572872 | tf_op jit(solution)/shard_map/ppermute | solution.py:12
  60.5 5.3 %collective-permute-done.4 = bf16[512,512]{0,1:T(8,128)(2,1)S(1)} collective-permute-done((bf16[512,512]{0,1:T(8,128)(2,1)S(1)}, bf16[512,512]{0,1:T(8,128)(2,1)S(1)}, u32[]{:S(2)}, u32[]{:S(2)}) %collective-permute-start.4) | collective-permute-done | bytes 524320 | tf_op jit(solution)/shard_map/ppermute | solution.py:12
  65.9 6.9 %collective-permute-done.5 = bf16[512,512]{0,1:T(8,128)(2,1)S(1)} collective-permute-done((bf16[512,512]{0,1:T(8,128)(2,1)S(1)}, bf16[512,512]{0,1:T(8,128)(2,1)S(1)}, u32[]{:S(2)}, u32[]{:S(2)}) %collective-permute-start.5) | collective-permute-done | bytes 524320 | tf_op jit(solution)/shard_map/ppermute | solution.py:12
  73.4 1.3 %collective-permute-start.6 = (bf16[1,16,512]{2,1,0:T(8,128)(2,1)S(1)}, bf16[1,16,512]{2,1,0:T(8,128)(2,1)S(1)}, u32[]{:S(2)}, u32[]{:S(2)}) collective-permute-start(bf16[1,16,512]{2,1,0:T(8,128)(2,1)S(1)} %get-tuple-element.19), channel_id=1, source_target_pairs={{0,16},{16,32},{32,48},{48,64},{64,80},{80,96},{96,112},{112,128},... | collective-permute-start | bytes 49160 | tf_op jit(solution)/shard_map/ppermute | solution.py:23
  74.7 1.3 %collective-permute-start.7 = (bf16[1,16,512]{2,1,0:T(8,128)(2,1)S(1)}, bf16[1,16,512]{2,1,0:T(8,128)(2,1)S(1)}, u32[]{:S(2)}, u32[]{:S(2)}) collective-permute-start(bf16[1,16,512]{2,1,0:T(8,128)(2,1)S(1)} %get-tuple-element.20), channel_id=1, source_target_pairs={{16,0},{32,16},{48,32},{64,48},{80,64},{96,80},{112,96},{128,112},... | collective-permute-start | bytes 49160 | tf_op jit(solution)/shard_map/ppermute | solution.py:25
  76.0 1.3 %fusion.20 = bf16[1024,512]{0,1:T(8,128)(2,1)S(1)} fusion(bf16[1024,512]{0,1:T(8,128)(2,1)S(1)} %constant_dynamic-update-slice_fusion, bf16[1,1,1024,1024]{3,2,1,0:T(8,128)(2,1)S(1)} %copy-done), kind=kOutput, calls=%fused_computation.12 | convolution fusion | flops 1074266112 | bytes 4194304 | tf_op jit(solution)/shard_map/dot_general | solution.py:34
  77.3 3.0 %collective-permute-done.7 = bf16[1,16,512]{2,1,0:T(8,128)(2,1)S(1)} collective-permute-done((bf16[1,16,512]{2,1,0:T(8,128)(2,1)S(1)}, bf16[1,16,512]{2,1,0:T(8,128)(2,1)S(1)}, u32[]{:S(2)}, u32[]{:S(2)}) %collective-permute-start.7) | collective-permute-done | bytes 16416 | tf_op jit(solution)/shard_map/ppermute | solution.py:25
  81.0 1.9 %collective-permute-start.8 = (bf16[18,1,512]{2,1,0:T(2,128)(2,1)}, bf16[18,1,512]{2,1,0:T(2,128)(2,1)S(1)}, u32[]{:S(2)}, u32[]{:S(2)}) collective-permute-start(bf16[18,1,512]{2,1,0:T(2,128)(2,1)} %get-tuple-element.17), channel_id=1, source_target_pairs={{0,1},{1,2},{2,3},{3,4},{4,5},{5,6},{6,7},{7,8},{8,9},{9,10},{10,1... | collective-permute-start | bytes 55304 | tf_op jit(solution)/shard_map/ppermute | solution.py:23
  83.0 6.0 %collective-permute-start.9 = (bf16[18,1,512]{2,1,0:T(2,128)(2,1)S(1)}, bf16[18,1,512]{2,1,0:T(2,128)(2,1)S(1)}, u32[]{:S(2)}, u32[]{:S(2)}) collective-permute-start(bf16[18,1,512]{2,1,0:T(2,128)(2,1)S(1)} %get-tuple-element.18), channel_id=1, source_target_pairs={{1,0},{2,1},{3,2},{4,3},{5,4},{6,5},{7,6},{8,7},{9,8},{10,9},{11,1... | collective-permute-start | bytes 55304 | tf_op jit(solution)/shard_map/ppermute | solution.py:25
  89.9 2.0 %copy.12 = bf16[1,1,512,512]{3,2,1,0:T(8,128)(2,1)} copy(bf16[1,1,512,512]{2,3,1,0:T(8,128)(2,1)} %get-tuple-element.9) | data formatting | bytes 1048576
  93.1 1.7 %fusion.42 = f32[16,16,512]{2,1,0:T(8,128)} fusion(f32[18,18,512]{2,1,0:T(8,128)S(1)} %maximum_convert_fusion, f32[16,16,512]{2,1,0:T(8,128)S(1)} %bitcast.48, f32[16,16]{1,0:T(8,128)} %select_reduce_fusion), kind=kLoop, calls=%fused_computation.27 | loop fusion | flops 917504 | bytes 3146752 | tf_op jit(solution)/shard_map/add | solution.py:68
  (23 shorter events, 4.4 us)
Async XLA Ops:
  0.6 1.6 %copy-start = (bf16[1,1,1024,1024]{3,2,1,0:T(8,128)(2,1)S(1)}, bf16[1,1,1024,1024]{3,2,1,0:T(8,128)(2,1)}, u32[]{:S(2)}) copy-start(bf16[1,1,1024,1024]{3,2,1,0:T(8,128)(2,1)} %param.6) | copy-start | bytes 6291460
  4.8 15.0 %collective-permute-start = (bf16[512,512]{0,1:T(8,128)(2,1)S(1)}, bf16[512,512]{0,1:T(8,128)(2,1)S(1)}, u32[]{:S(2)}, u32[]{:S(2)}) collective-permute-start(bf16[512,512]{0,1:T(8,128)(2,1)S(1)} %get-tuple-element.15), channel_id=1, source_target_pairs={{0,16},{16,32},{32,48},{48,64},{64,80},{80,96},{96,112},{112,128},... | collective-permute-start | bytes 1572872 | tf_op jit(solution)/shard_map/ppermute | solution.py:12
  8.7 24.1 %collective-permute-start.1 = (bf16[512,512]{0,1:T(8,128)(2,1)S(1)}, bf16[512,512]{0,1:T(8,128)(2,1)S(1)}, u32[]{:S(2)}, u32[]{:S(2)}) collective-permute-start(bf16[512,512]{0,1:T(8,128)(2,1)S(1)} %get-tuple-element.16), channel_id=1, source_target_pairs={{0,1},{1,2},{2,3},{3,4},{4,5},{5,6},{6,7},{7,8},{8,9},{9,10},{10,1... | collective-permute-start | bytes 1572872 | tf_op jit(solution)/shard_map/ppermute | solution.py:12
  34.2 11.2 %collective-permute-start.2 = (bf16[512,512]{0,1:T(8,128)(2,1)S(1)}, bf16[512,512]{0,1:T(8,128)(2,1)S(1)}, u32[]{:S(2)}, u32[]{:S(2)}) collective-permute-start(bf16[512,512]{0,1:T(8,128)(2,1)S(1)} %get-tuple-element.13), channel_id=1, source_target_pairs={{0,16},{16,32},{32,48},{48,64},{64,80},{80,96},{96,112},{112,128},... | collective-permute-start | bytes 1572872 | tf_op jit(solution)/shard_map/ppermute | solution.py:12
  35.5 19.4 %collective-permute-start.3 = (bf16[512,512]{0,1:T(8,128)(2,1)S(1)}, bf16[512,512]{0,1:T(8,128)(2,1)S(1)}, u32[]{:S(2)}, u32[]{:S(2)}) collective-permute-start(bf16[512,512]{0,1:T(8,128)(2,1)S(1)} %get-tuple-element.14), channel_id=1, source_target_pairs={{0,1},{1,2},{2,3},{3,4},{4,5},{5,6},{6,7},{7,8},{8,9},{9,10},{10,1... | collective-permute-start | bytes 1572872 | tf_op jit(solution)/shard_map/ppermute | solution.py:12
  56.2 3.5 %copy-start.2 = (s32[16,16]{1,0:T(8,128)S(1)}, s32[16,16]{1,0:T(8,128)}, u32[]{:S(2)}) copy-start(s32[16,16]{1,0:T(8,128)} %param.10) | copy-start | bytes 3076
  56.2 3.5 %copy-start.3 = (f32[16]{0:T(128)S(1)}, f32[16]{0:T(128)}, u32[]{:S(2)}) copy-start(f32[16]{0:T(128)} %param.11) | copy-start | bytes 196
  56.2 16.6 %copy-start.1 = (bf16[1,1,256,1024]{3,2,1,0:T(8,128)(2,1)S(1)}, bf16[1,1,256,1024]{3,2,1,0:T(8,128)(2,1)}, u32[]{:S(2)}) copy-start(bf16[1,1,256,1024]{3,2,1,0:T(8,128)(2,1)} %param.7) | copy-start | bytes 1572868
  56.3 9.5 %collective-permute-start.4 = (bf16[512,512]{0,1:T(8,128)(2,1)S(1)}, bf16[512,512]{0,1:T(8,128)(2,1)S(1)}, u32[]{:S(2)}, u32[]{:S(2)}) collective-permute-start(bf16[512,512]{0,1:T(8,128)(2,1)S(1)} %get-tuple-element.12), channel_id=1, source_target_pairs={{0,16},{16,32},{32,48},{48,64},{64,80},{80,96},{96,112},{112,128},... | collective-permute-start | bytes 1572872 | tf_op jit(solution)/shard_map/ppermute | solution.py:12
  57.8 15.0 %collective-permute-start.5 = (bf16[512,512]{0,1:T(8,128)(2,1)S(1)}, bf16[512,512]{0,1:T(8,128)(2,1)S(1)}, u32[]{:S(2)}, u32[]{:S(2)}) collective-permute-start(bf16[512,512]{0,1:T(8,128)(2,1)S(1)} %get-tuple-element.11), channel_id=1, source_target_pairs={{0,1},{1,2},{2,3},{3,4},{4,5},{5,6},{6,7},{7,8},{8,9},{9,10},{10,1... | collective-permute-start | bytes 1572872 | tf_op jit(solution)/shard_map/ppermute | solution.py:12
  73.4 3.9 %collective-permute-start.6 = (bf16[1,16,512]{2,1,0:T(8,128)(2,1)S(1)}, bf16[1,16,512]{2,1,0:T(8,128)(2,1)S(1)}, u32[]{:S(2)}, u32[]{:S(2)}) collective-permute-start(bf16[1,16,512]{2,1,0:T(8,128)(2,1)S(1)} %get-tuple-element.19), channel_id=1, source_target_pairs={{0,16},{16,32},{32,48},{48,64},{64,80},{80,96},{96,112},{112,128},... | collective-permute-start | bytes 49160 | tf_op jit(solution)/shard_map/ppermute | solution.py:23
  74.7 5.6 %collective-permute-start.7 = (bf16[1,16,512]{2,1,0:T(8,128)(2,1)S(1)}, bf16[1,16,512]{2,1,0:T(8,128)(2,1)S(1)}, u32[]{:S(2)}, u32[]{:S(2)}) collective-permute-start(bf16[1,16,512]{2,1,0:T(8,128)(2,1)S(1)} %get-tuple-element.20), channel_id=1, source_target_pairs={{16,0},{32,16},{48,32},{64,48},{80,64},{96,80},{112,96},{128,112},... | collective-permute-start | bytes 49160 | tf_op jit(solution)/shard_map/ppermute | solution.py:25
  81.0 11.9 %collective-permute-start.8 = (bf16[18,1,512]{2,1,0:T(2,128)(2,1)}, bf16[18,1,512]{2,1,0:T(2,128)(2,1)S(1)}, u32[]{:S(2)}, u32[]{:S(2)}) collective-permute-start(bf16[18,1,512]{2,1,0:T(2,128)(2,1)} %get-tuple-element.17), channel_id=1, source_target_pairs={{0,1},{1,2},{2,3},{3,4},{4,5},{5,6},{6,7},{7,8},{8,9},{9,10},{10,1... | collective-permute-start | bytes 55304 | tf_op jit(solution)/shard_map/ppermute | solution.py:23
  83.0 10.0 %collective-permute-start.9 = (bf16[18,1,512]{2,1,0:T(2,128)(2,1)S(1)}, bf16[18,1,512]{2,1,0:T(2,128)(2,1)S(1)}, u32[]{:S(2)}, u32[]{:S(2)}) collective-permute-start(bf16[18,1,512]{2,1,0:T(2,128)(2,1)S(1)} %get-tuple-element.18), channel_id=1, source_target_pairs={{1,0},{2,1},{3,2},{4,3},{5,4},{6,5},{7,6},{8,7},{9,8},{10,9},{11,1... | collective-permute-start | bytes 55304 | tf_op jit(solution)/shard_map/ppermute | solution.py:25
where the time goes:
time: 95.4 us; the launch traced here: 94.8 us
  waiting for transfers between devices  54.9 us (58%)
  starting transfers between devices  22.9 us (24%)
  matrix products  6.82 us (7%)
  local copies, waits for them, and re-layouts  5.86 us (6%)
  other arithmetic  3.42 us (4%)
    ppermute x6, waiting for transfers between devices, from_behind(): return lax.ppermute(block, axis, route)  51.9 us
    ppermute x6, starting transfers between devices, from_behind(): return lax.ppermute(block, axis, route)  12.4 us
    ppermute x2, starting transfers between devices, extended(): lax.ppermute(head, axis, [((i + 1) % count, i) for i in range(ends)])  7.34 us
    dot_general x4, matrix products, advance(): jnp.dot(mapping, stacked, preferred_element_type=jnp.float32)  6.34 us
    unnamed x11, local copies, waits for them, and re-layouts  4.71 us
    ppermute x2, starting transfers between devices, extended(): lax.ppermute(tail, axis, [(i, (i + 1) % count) for i in range(ends)])  3.2 us
    ppermute x2, waiting for transfers between devices, extended(): lax.ppermute(head, axis, [((i + 1) % count, i) for i in range(ends)])  3.03 us
  transfers between devices with their start and end apart: 10, of which 7 were waited for; matrix products, arithmetic and copies ran while one was open for 6% of the time, Pallas kernels for 0%

commit v1 on v0

v1 whole, which is shorter than its diff:
```python
import functools

import jax
import jax.numpy as jnp
from jax import lax
from jax.experimental import pallas as pl
from jax.experimental.pallas import tpu as pltpu
from jax.sharding import PartitionSpec as P

MESH = pl.DeviceIdType.MESH
STEPS = 4
LANES = 128
BY_WAY = (0, 2)


def remote(src, dst, send_sem, recv_sem, device):
    return pltpu.make_async_remote_copy(
        src_ref=src, dst_ref=dst, send_sem=send_sem, recv_sem=recv_sem,
        device_id=device, device_id_type=MESH,
    )


def sweep(
    n_gx, n_gy,
    impedance, rebuild_map, left, lower, kinds_hbm, wavenum_hbm,
    right_out, upper_out, residual,
    amap, bmap, traces, outgoing, way, volume, factor, beside, edge_out, edge_in,
    cell_kind, kind_wavenum, load_sem, map_sem, right_send, right_recv, upper_send, upper_recv, way_send, way_recv, edge_send, edge_recv,
):
    gx, gy = lax.axis_index("gx"), lax.axis_index("gy")
    rows = left.shape[0]
    chunks = left.shape[1] // LANES
    cells = rebuild_map.shape[0]
    cx, cy = cell_kind.shape
    half, last_x, last_y = n_gx // 2, n_gx - 1, n_gy - 1
    behind, ahead = lax.rem(gx + last_x, n_gx), lax.rem(gx + 1, n_gx)
    below, above = lax.rem(gy + last_y, n_gy), lax.rem(gy + 1, n_gy)

    def map_load(k):
        part = pl.ds(k * rows, rows)
        return pltpu.make_async_copy(impedance.at[part, :], amap.at[part, :], map_sem.at[k])

    def rebuild_load():
        return pltpu.make_async_copy(rebuild_map, bmap, map_sem.at[2])

    def kinds_load():
        return pltpu.make_async_copy(kinds_hbm, cell_kind, map_sem.at[3])

    def wavenum_load():
        return pltpu.make_async_copy(wavenum_hbm, kind_wavenum, map_sem.at[4])

    def trace_load(side, c):
        source = (left, lower)[side]
        return pltpu.make_async_copy(
            source.at[:, pl.ds(c * LANES, LANES)], traces.at[0, c, pl.ds(side * rows, rows), :], load_sem.at[side, c]
        )

    barrier = pltpu.get_barrier_semaphore()
    for device in ((behind, gy), (ahead, gy), (gx, below), (gx, above)):
        pl.semaphore_signal(barrier, inc=1, device_id=device, device_id_type=MESH)

    @pl.when((gx == half - 1) | (gx == half))
    def _():
        pl.semaphore_signal(barrier, inc=1, device_id=(last_x, gy), device_id_type=MESH)

    @pl.when(gx == last_x)
    def _():
        pl.semaphore_signal(barrier, inc=1, device_id=(half - 1, gy), device_id_type=MESH)
        pl.semaphore_signal(barrier, inc=1, device_id=(half, gy), device_id_type=MESH)

    map_load(0).start()
    for side in (0, 1):
        trace_load(side, 0).start()
    map_load(1).start()
    for c in range(1, chunks):
        for side in (0, 1):
            trace_load(side, c).start()
    rebuild_load().start()
    kinds_load().start()
    wavenum_load().start()

    def to_right(s, c):
        return remote(
            outgoing.at[s, c, pl.ds(0, rows), :], traces.at[s + 1, c, pl.ds(0, rows), :],
            right_send.at[s, c], right_recv.at[s, c], (ahead, gy),
        )

    def to_way(s, c):
        return remote(
            outgoing.at[s, c, pl.ds(0, rows), :], way.at[s, c], right_send.at[s, c], way_recv.at[s, c], (last_x, gy)
        )

    def from_way(s, c):
        return remote(
            way.at[s, c], traces.at[s + 1, c, pl.ds(0, rows), :], way_send.at[s, c], right_recv.at[s, c], (half, gy)
        )

    def to_upper(s, c):
        return remote(
            outgoing.at[s, c, pl.ds(rows, rows), :], traces.at[s + 1, c, pl.ds(rows, rows), :],
            upper_send.at[s, c], upper_recv.at[s, c], (gx, above),
        )

    def is_way(c):
        found = c == BY_WAY[0]
        for k in BY_WAY[1:]:
            found = found | (c == k)
        return found

    def send_right(s, c):
        by_way = (gx == half - 1) & is_way(c)

        @pl.when((gx < last_x) & jnp.logical_not(by_way))
        def _():
            to_right(s, c).start()

        @pl.when(by_way)
        def _():
            to_way(s, c).start()

    def arrived(s, c):
        @pl.when(gx > 0)
        def _():
            to_right(s, c).wait_recv()

        @pl.when((gx == last_x) & is_way(c))
        def _():
            to_way(s, c).wait_recv()
            from_way(s, c).start()

        @pl.when(gy > 0)
        def _():
            to_upper(s, c).wait_recv()

    def part(k, s, c):
        return jnp.dot(
            amap[pl.ds(k * rows, rows), :], traces[s, c], preferred_element_type=jnp.float32
        ).astype(jnp.bfloat16)

    def send_upper(s, c):
        @pl.when(gy < last_y)
        def _():
            to_upper(s, c).start()

    def advance(s, c):
        outgoing[s, c, pl.ds(0, rows), :] = part(0, s, c)
        send_right(s, c)
        outgoing[s, c, pl.ds(rows, rows), :] = part(1, s, c)
        send_upper(s, c)

    map_load(0).wait()
    for side in (0, 1):
        trace_load(side, 0).wait()
    outgoing[0, 0, pl.ds(0, rows), :] = part(0, 0, 0)
    greeted = jnp.where(gx == last_x, 6, jnp.where((gx == half - 1) | (gx == half), 5, 4))
    pl.semaphore_wait(barrier, greeted)
    send_right(0, 0)
    map_load(1).wait()
    outgoing[0, 0, pl.ds(rows, rows), :] = part(1, 0, 0)
    send_upper(0, 0)

    @pl.loop(1, chunks)
    def _(c):
        trace_load(0, c).wait()
        trace_load(1, c).wait()
        advance(0, c)

    def clear(side):
        @pl.loop(1, STEPS)
        def _(s):
            @pl.loop(0, chunks)
            def _(c):
                traces[s, c, pl.ds(side * rows, rows), :] = jnp.zeros((rows, LANES), traces.dtype)

    def clear_edge(k):
        edge_in[k] = jnp.zeros(edge_in.shape[1:], edge_in.dtype)

    @pl.when(gx == 0)
    def _():
        clear(0)
        clear_edge(0)

    @pl.when(gx == last_x)
    def _():
        clear_edge(1)

    @pl.when(gy == 0)
    def _():
        clear(1)
        clear_edge(2)

    @pl.when(gy == last_y)
    def _():
        clear_edge(3)

    kinds_load().wait()
    wavenum_load().wait()

    @pl.loop(0, cx)
    def _(a):
        @pl.loop(0, cy)
        def _(b):
            factor[pl.ds(a * cy + b, 1), :] = jnp.full((1, LANES), kind_wavenum[cell_kind[a, b]] - 4.0, jnp.float32)

    @pl.loop(1, STEPS - 1)
    def _(s):
        @pl.loop(0, chunks)
        def _(c):
            arrived(s - 1, c)
            advance(s, c)

    rebuild_load().wait()
    reach = (
        (gx > 0, gx < last_x, (ahead, gy)),
        (gx < last_x, gx > 0, (behind, gy)),
        (gy > 0, gy < last_y, (gx, above)),
        (gy < last_y, gy > 0, (gx, below)),
    )

    def edge_copy(k, c):
        return remote(
            edge_out.at[k, c], edge_in.at[k, c], edge_send.at[k, c], edge_recv.at[k, c], reach[k][2]
        )

    def rebuild(c):
        volume[c] = jnp.dot(bmap[...], traces[STEPS - 1, c], preferred_element_type=jnp.float32)
        edge_out[0, c] = volume[c, pl.ds(cells - cy, cy), :].astype(edge_out.dtype)
        edge_out[1, c] = volume[c, pl.ds(0, cy), :].astype(edge_out.dtype)
        edge_out[2, c] = volume[c, pl.ds(cy - 1, cx, stride=cy), :].astype(edge_out.dtype)
        edge_out[3, c] = volume[c, pl.ds(0, cx, stride=cy), :].astype(edge_out.dtype)
        for k in range(4):
            @pl.when(reach[k][1])
            def _(k=k):
                edge_copy(k, c).start()

    def finish(c):
        for k in range(4):
            @pl.when(reach[k][0])
            def _(k=k):
                edge_copy(k, c).wait_recv()
        cell = volume[c]
        beside[0] = pltpu.roll(cell, 1, 0)
        beside[1] = pltpu.roll(cell, cells - 1, 0)
        beside[0, pl.ds(0, cx, stride=cy), :] = edge_in[2, c].astype(jnp.float32)
        beside[1, pl.ds(cy - 1, cx, stride=cy), :] = edge_in[3, c].astype(jnp.float32)
        along_x = jnp.concatenate([edge_in[0, c].astype(jnp.float32), cell[: cells - cy]], axis=0) + jnp.concatenate(
            [cell[cy:], edge_in[1, c].astype(jnp.float32)], axis=0
        )
        residual[:, pl.ds(pl.multiple_of(c * LANES, LANES), LANES)] = (
            along_x + beside[0] + beside[1] + factor[...] * cell
        )

    @pl.loop(0, chunks)
    def _(c):
        arrived(STEPS - 2, c)
        rebuild(c)
        lanes = pl.ds(pl.multiple_of(c * LANES, LANES), LANES)
        right_out[:, lanes] = part(0, STEPS - 1, c)
        upper_out[:, lanes] = part(1, STEPS - 1, c)

        @pl.when(c > 0)
        def _():
            finish(c - 1)

    finish(chunks - 1)

    @pl.loop(0, STEPS - 1)
    def _(s):
        @pl.loop(0, chunks)
        def _(c):
            @pl.when(gx < last_x)
            def _():
                to_right(s, c).wait_send()

            @pl.when((gx == last_x) & is_way(c))
            def _():
                from_way(s, c).wait_send()

            @pl.when(gy < last_y)
            def _():
                to_upper(s, c).wait_send()

    @pl.loop(0, chunks)
    def _(c):
        for k in range(4):
            @pl.when(reach[k][1])
            def _(k=k):
                edge_copy(k, c).wait_send()


def per_device(n_gx, n_gy, impedance, rebuild_map, left_trace, lower_trace, cell_kind, kind_wavenum):
    rows, sources = left_trace.shape[2:]
    cells = rebuild_map.shape[2]
    cx, cy = cell_kind.shape
    chunks = sources // LANES
    bf16, f32 = jnp.bfloat16, jnp.float32
    pair = lambda *shape: [pltpu.SemaphoreType.DMA(shape)] * 2
    right, upper, residual = pl.pallas_call(
        functools.partial(sweep, n_gx, n_gy),
        out_shape=(
            pltpu.VMEM((rows, sources), bf16),
            pltpu.VMEM((rows, sources), bf16),
            pltpu.VMEM((cells, sources), f32),
        ),
        in_specs=[pl.BlockSpec(memory_space=pltpu.HBM)] * 6,
        out_specs=[pl.BlockSpec(memory_space=pltpu.VMEM)] * 3,
        scratch_shapes=[
            pltpu.VMEM((2 * rows, 2 * rows), bf16),
            pltpu.VMEM((cells, 2 * rows), bf16),
            pltpu.VMEM((STEPS, chunks, 2 * rows, LANES), bf16),
            pltpu.VMEM((STEPS - 1, chunks, 2 * rows, LANES), bf16),
            pltpu.VMEM((STEPS - 1, chunks, rows, LANES), bf16),
            pltpu.VMEM((chunks, cells, LANES), f32),
            pltpu.VMEM((cells, LANES), f32),
            pltpu.VMEM((2, cells, LANES), f32),
            pltpu.VMEM((4, chunks, cy, LANES), bf16),
            pltpu.VMEM((4, chunks, cy, LANES), bf16),
            pltpu.SMEM((cx, cy), jnp.int32),
            pltpu.SMEM(kind_wavenum.shape, f32),
            pltpu.SemaphoreType.DMA((2, chunks)),
            pltpu.SemaphoreType.DMA((5,)),
            *pair(STEPS - 1, chunks),
            *pair(STEPS - 1, chunks),
            *pair(STEPS - 1, chunks),
            *pair(4, chunks),
        ],
        compiler_params=pltpu.CompilerParams(
            collective_id=0, has_side_effects=True, vmem_limit_bytes=40 * 2**20
        ),
        cost_estimate=pl.CostEstimate(flops=4_600_000_000, bytes_accessed=5_300_000, transcendentals=0),
        name="sweep",
    )(*[
        pltpu.with_memory_space_constraint(array, pltpu.HBM)
        for array in (impedance[0, 0], rebuild_map[0, 0], left_trace[0, 0], lower_trace[0, 0], cell_kind, kind_wavenum)
    ])
    return right[None, None], upper[None, None], residual.reshape(cx, cy, sources)


def solution(mesh):
    return jax.shard_map(
        functools.partial(per_device, mesh.shape["gx"], mesh.shape["gy"]),
        mesh=mesh,
        in_specs=(
            P("gx", "gy", None, None),
            P("gx", "gy", None, None),
            P("gx", "gy", None, None),
            P("gx", "gy", None, None),
            P("gx", "gy"),
            P(),
        ),
        out_specs=(P("gx", "gy", None, None), P("gx", "gy", None, None), P("gx", "gy", None)),
        check_vma=False,
    )
```

time: 95.4 us -> 61.5 us (0.64)
  the two profiles are of different devices: /device:TPU:24 before, /device:TPU:11 now
where the time goes in v1:
time: 61.5 us; the launch traced here: 61.4 us
  Pallas kernels  58.3 us (95%)
  local copies, waits for them, and re-layouts  2.38 us (4%)
  between operations  0.64 us (1%)
    pallas_call x1, Pallas kernels, per_device(): pl.pallas_call(functools.partial(sweep, n_gx, n_gy), out_shape=(pltpu.VME...  58.3 us
    unnamed x3, local copies, waits for them, and re-layouts  2.38 us

profile of v1, /device:TPU:11, one launch (start us, length us, event | category | flops | bytes accessed | tf_op | source)
XLA Modules:
  0.0 61.4 jit_solution(15488509524288403133)
XLA Ops:
  0.6 58.3 %sweep.1 = (bf16[512,512]{1,0:T(8,128)(2,1)S(1)}, bf16[512,512]{1,0:T(8,128)(2,1)S(1)}, f32[256,512]{1,0:T(8,128)S(1)}) custom-call(bf16[1024,1024]{1,0:T(8,128)(2,1)} %bitcast.10, bf16[256,1024]{1,0:T(8,128)(2,1)} %bitcast.11, bf16[512,512]{1,0:T(8,128)(2,1)} %bitcast.12, bf16[512,512]{1,0:T(8,128)(2,1)} %bitcast.13, s32[16,16]{1,0:T(8,128)} %kinds_hbm.1, ...), custom_call_target="tpu_custom_call" | custom-call | flops 4600000000 | bytes 5300000 | tf_op jit(solution)/shard_map/sweep/pallas_call | solution.py:298
  59.0 0.8 %copy.12 = bf16[1,1,512,512]{3,2,1,0:T(8,128)(2,1)} copy(bf16[1,1,512,512]{3,2,1,0:T(8,128)(2,1)S(1)} %bitcast.9) | data formatting | bytes 1048576
  59.8 0.8 %copy.13 = bf16[1,1,512,512]{3,2,1,0:T(8,128)(2,1)} copy(bf16[1,1,512,512]{3,2,1,0:T(8,128)(2,1)S(1)} %bitcast.8) | data formatting | bytes 1048576
  60.6 0.8 %copy.14 = f32[16,16,512]{2,1,0:T(8,128)} copy(f32[16,16,512]{2,1,0:T(8,128)S(1)} %bitcast.7) | data formatting | bytes 1048576

commit v2 on v1

v2 whole, which is shorter than its diff:
```python
import functools

import jax
import jax.numpy as jnp
from jax import lax
from jax.experimental import pallas as pl
from jax.experimental.pallas import tpu as pltpu
from jax.sharding import PartitionSpec as P

MESH = pl.DeviceIdType.MESH
STEPS = 4
LANES = 128

def remote(src, dst, send_sem, recv_sem, device):
    return pltpu.make_async_remote_copy(
        src_ref=src, dst_ref=dst, send_sem=send_sem, recv_sem=recv_sem,
        device_id=device, device_id_type=MESH,
    )


def sweep(
    n_gx, n_gy,
    impedance, rebuild_map, left, lower, kinds_hbm, wavenum_hbm,
    right_out, upper_out, residual,
    amap, bmap, traces, outgoing, way, emap, factor, beside, edge_out, edge_in,
    cell_kind, kind_wavenum, load_sem, map_sem, right_send, right_recv, upper_send, upper_recv, way_send, way_recv, edge_send, edge_recv,
):
    gx, gy = lax.axis_index("gx"), lax.axis_index("gy")
    rows = left.shape[0]
    chunks = left.shape[1] // LANES
    cells = rebuild_map.shape[0]
    cx, cy = cell_kind.shape
    half, last_x, last_y = n_gx // 2, n_gx - 1, n_gy - 1
    behind, ahead = lax.rem(gx + last_x, n_gx), lax.rem(gx + 1, n_gx)
    below, above = lax.rem(gy + last_y, n_gy), lax.rem(gy + 1, n_gy)

    quarter = rows // 2

    def map_load(k):
        part = pl.ds(k * quarter, quarter)
        return pltpu.make_async_copy(impedance.at[part, :], amap.at[part, :], map_sem.at[k])

    def rebuild_load():
        return pltpu.make_async_copy(rebuild_map, bmap, map_sem.at[6])

    def kinds_load():
        return pltpu.make_async_copy(kinds_hbm, cell_kind, map_sem.at[4])

    def wavenum_load():
        return pltpu.make_async_copy(wavenum_hbm, kind_wavenum, map_sem.at[5])

    def trace_load(side, c):
        source = (left, lower)[side]
        return pltpu.make_async_copy(
            source.at[:, pl.ds(c * LANES, LANES)], traces.at[0, c, pl.ds(side * rows, rows), :], load_sem.at[side, c]
        )

    for side in (0, 1):
        trace_load(side, 0).start()
    for k in range(4):
        map_load(k).start()
    for c in range(1, chunks):
        for side in (0, 1):
            trace_load(side, c).start()
    rebuild_load().start()
    kinds_load().start()
    wavenum_load().start()

    barrier = pltpu.get_barrier_semaphore()
    senders = (
        (gx > 0, (behind, gy)),
        (gy > 0, (gx, below)),
        (gx == last_x, (half - 1, gy)),
        (gx == half, (last_x, gy)),
    )
    for present, device in senders:
        @pl.when(present)
        def _(device=device):
            pl.semaphore_signal(barrier, inc=1, device_id=device, device_id_type=MESH)

    greeted = 0
    for present in (gx < last_x, gy < last_y, gx == half - 1, gx == last_x):
        greeted = greeted + jnp.where(present, 1, 0)

    def to_right(s, c):
        return remote(
            outgoing.at[s, c, pl.ds(0, rows), :], traces.at[s + 1, c, pl.ds(0, rows), :],
            right_send.at[s, c], right_recv.at[s, c], (ahead, gy),
        )

    def to_way(s, c):
        return remote(
            outgoing.at[s, c, pl.ds(0, rows), :], way.at[s, c], right_send.at[s, c], way_recv.at[s, c], (last_x, gy)
        )

    def from_way(s, c):
        return remote(
            way.at[s, c], traces.at[s + 1, c, pl.ds(0, rows), :], way_send.at[s, c], right_recv.at[s, c], (half, gy)
        )

    def to_upper(s, c):
        return remote(
            outgoing.at[s, c, pl.ds(rows, rows), :], traces.at[s + 1, c, pl.ds(rows, rows), :],
            upper_send.at[s, c], upper_recv.at[s, c], (gx, above),
        )

    def is_way(s, c):
        return ((s == 0) & (c >= chunks // 2)) | ((s == 1) & (lax.rem(c, 2) == 0))

    def send_right(s, c):
        by_way = (gx == half - 1) & is_way(s, c)

        @pl.when((gx < last_x) & jnp.logical_not(by_way))
        def _():
            to_right(s, c).start()

        @pl.when(by_way)
        def _():
            to_way(s, c).start()

    def arrived(s, c):
        @pl.when(gx > 0)
        def _():
            to_right(s, c).wait_recv()

        @pl.when(gy > 0)
        def _():
            to_upper(s, c).wait_recv()

    def relay(s, c):
        @pl.when((gx == last_x) & is_way(s, c))
        def _():
            to_way(s, c).wait_recv()
            from_way(s, c).start()

    def multiply(s, c):
        return jnp.dot(amap[...], traces[s, c], preferred_element_type=jnp.float32).astype(jnp.bfloat16)

    def send_upper(s, c):
        @pl.when(gy < last_y)
        def _():
            to_upper(s, c).start()

    def advance(s, c):
        outgoing[s, c] = multiply(s, c)
        send_right(s, c)
        send_upper(s, c)

    for side in (0, 1):
        trace_load(side, 0).wait()
    for k in range(4):
        map_load(k).wait()
        part = pl.ds(k * quarter, quarter)
        outgoing[0, 0, part, :] = jnp.dot(
            amap[part, :], traces[0, 0], preferred_element_type=jnp.float32
        ).astype(jnp.bfloat16)
        if k == 1:
            pl.semaphore_wait(barrier, greeted)
            send_right(0, 0)
    send_upper(0, 0)

    @pl.loop(1, chunks)
    def _(c):
        trace_load(0, c).wait()
        trace_load(1, c).wait()
        advance(0, c)

    def clear(side):
        @pl.loop(1, STEPS)
        def _(s):
            @pl.loop(0, chunks)
            def _(c):
                traces[s, c, pl.ds(side * rows, rows), :] = jnp.zeros((rows, LANES), traces.dtype)

    def clear_edge(k):
        edge_in[:, pl.ds(k * cy, cy), :] = jnp.zeros((chunks, cy, LANES), edge_in.dtype)

    @pl.when(gx == 0)
    def _():
        clear(0)
        clear_edge(0)

    @pl.when(gx == last_x)
    def _():
        clear_edge(1)

    @pl.when(gy == 0)
    def _():
        clear(1)
        clear_edge(2)

    @pl.when(gy == last_y)
    def _():
        clear_edge(3)

    rebuild_load().wait()
    row = lax.broadcasted_iota(jnp.int32, (4 * cy, cells), 0)
    side, along = lax.div(row, cy), lax.rem(row, cy)
    chosen = jnp.where(
        side == 0, cells - cy + along, jnp.where(side == 1, along, jnp.where(side == 2, along * cy + cy - 1, along * cy))
    )
    chosen = lax.broadcasted_iota(jnp.int32, (4 * cy, cells), 1) == chosen
    emap[...] = jnp.dot(
        jnp.where(chosen, 1.0, 0.0).astype(jnp.bfloat16), bmap[...], preferred_element_type=jnp.float32
    ).astype(jnp.bfloat16)

    @pl.loop(1, STEPS - 1)
    def _(s):
        @pl.loop(0, chunks)
        def _(c):
            arrived(s - 1, c)
            advance(s, c)

            @pl.when((s == 1) & (c < chunks // 2))
            def _():
                relay(0, c + chunks // 2)

            @pl.when((s == 1) & (c == chunks // 2))
            def _():
                relay(1, 0)

            @pl.when((s == 2) & (c == 0))
            def _():
                relay(1, chunks // 2)

    reach = (
        (gx > 0, gx < last_x, (ahead, gy)),
        (gx < last_x, gx > 0, (behind, gy)),
        (gy > 0, gy < last_y, (gx, above)),
        (gy < last_y, gy > 0, (gx, below)),
    )

    def edge_copy(k, c):
        part = pl.ds(k * cy, cy)
        return remote(
            edge_out.at[c, part, :], edge_in.at[c, part, :], edge_send.at[k, c], edge_recv.at[k, c], reach[k][2]
        )

    def send_edges(c):
        edge_out[c] = jnp.dot(
            emap[...], traces[STEPS - 1, c], preferred_element_type=jnp.float32
        ).astype(edge_out.dtype)
        for k in range(4):
            @pl.when(reach[k][1])
            def _(k=k):
                edge_copy(k, c).start()

    first, last = pl.ds(0, cx, stride=cy), pl.ds(cy - 1, cx, stride=cy)

    def rebuild(c):
        cell = jnp.dot(bmap[...], traces[STEPS - 1, c], preferred_element_type=jnp.float32)
        none = jnp.zeros((cy, LANES), jnp.float32)
        beside[0] = pltpu.roll(cell, 1, 0)
        beside[1] = pltpu.roll(cell, cells - 1, 0)
        beside[0, first, :] = none
        beside[1, last, :] = none
        along_x = jnp.concatenate([none, cell[: cells - cy]], axis=0) + jnp.concatenate([cell[cy:], none], axis=0)
        residual[c] = along_x + beside[0] + beside[1] + factor[...] * cell

    def finish(c):
        for k in range(4):
            @pl.when(reach[k][0])
            def _(k=k):
                edge_copy(k, c).wait_recv()
        for k, part in enumerate((pl.ds(0, cy), pl.ds(cells - cy, cy), first, last)):
            residual[c, part, :] += edge_in[c, pl.ds(k * cy, cy), :].astype(jnp.float32)

    @pl.loop(0, chunks)
    def _(c):
        arrived(STEPS - 2, c)
        send_edges(c)

        @pl.when(c == 0)
        def _():
            kinds_load().wait()
            wavenum_load().wait()

            @pl.loop(0, cx)
            def _(a):
                for b in range(cy):
                    factor[pl.ds(a * cy + b, 1), :] = jnp.full(
                        (1, LANES), kind_wavenum[cell_kind[a, b]] - 4.0, jnp.float32
                    )

        rebuild(c)
        lanes = pl.ds(pl.multiple_of(c * LANES, LANES), LANES)
        leaving = multiply(STEPS - 1, c)
        right_out[:, lanes] = leaving[:rows]
        upper_out[:, lanes] = leaving[rows:]

        @pl.when(c > 0)
        def _():
            finish(c - 1)

    finish(chunks - 1)

    @pl.loop(0, STEPS - 1)
    def _(s):
        @pl.loop(0, chunks)
        def _(c):
            @pl.when(gx < last_x)
            def _():
                to_right(s, c).wait_send()

            @pl.when((gx == last_x) & is_way(s, c))
            def _():
                from_way(s, c).wait_send()

            @pl.when(gy < last_y)
            def _():
                to_upper(s, c).wait_send()

    @pl.loop(0, chunks)
    def _(c):
        for k in range(4):
            @pl.when(reach[k][1])
            def _(k=k):
                edge_copy(k, c).wait_send()


def flush(right, upper, residual, right_out, upper_out, residual_out, sem):
    copies = [
        pltpu.make_async_copy(right, right_out, sem.at[0]),
        pltpu.make_async_copy(upper, upper_out, sem.at[1]),
    ]
    for c in range(residual.shape[0]):
        lanes = pl.ds(c * LANES, LANES)
        copies.append(pltpu.make_async_copy(residual.at[c], residual_out.at[:, lanes], sem.at[2 + c]))
    for copy in copies:
        copy.start()
    for copy in copies:
        copy.wait()


def per_device(n_gx, n_gy, impedance, rebuild_map, left_trace, lower_trace, cell_kind, kind_wavenum):
    rows, sources = left_trace.shape[2:]
    cells = rebuild_map.shape[2]
    cx, cy = cell_kind.shape
    chunks = sources // LANES
    bf16, f32 = jnp.bfloat16, jnp.float32
    pair = lambda *shape: [pltpu.SemaphoreType.DMA(shape)] * 2
    right, upper, residual = pl.pallas_call(
        functools.partial(sweep, n_gx, n_gy),
        out_shape=(
            pltpu.VMEM((rows, sources), bf16),
            pltpu.VMEM((rows, sources), bf16),
            pltpu.VMEM((chunks, cells, LANES), f32),
        ),
        in_specs=[pl.BlockSpec(memory_space=pltpu.HBM)] * 6,
        out_specs=[pl.BlockSpec(memory_space=pltpu.VMEM)] * 3,
        scratch_shapes=[
            pltpu.VMEM((2 * rows, 2 * rows), bf16),
            pltpu.VMEM((cells, 2 * rows), bf16),
            pltpu.VMEM((STEPS, chunks, 2 * rows, LANES), bf16),
            pltpu.VMEM((STEPS - 1, chunks, 2 * rows, LANES), bf16),
            pltpu.VMEM((STEPS - 1, chunks, rows, LANES), bf16),
            pltpu.VMEM((4 * cy, 2 * rows), bf16),
            pltpu.VMEM((cells, LANES), f32),
            pltpu.VMEM((2, cells, LANES), f32),
            pltpu.VMEM((chunks, 4 * cy, LANES), bf16),
            pltpu.VMEM((chunks, 4 * cy, LANES), bf16),
            pltpu.SMEM((cx, cy), jnp.int32),
            pltpu.SMEM(kind_wavenum.shape, f32),
            pltpu.SemaphoreType.DMA((2, chunks)),
            pltpu.SemaphoreType.DMA((7,)),
            *pair(STEPS - 1, chunks),
            *pair(STEPS - 1, chunks),
            *pair(STEPS - 1, chunks),
            *pair(4, chunks),
        ],
        compiler_params=pltpu.CompilerParams(
            collective_id=0, has_side_effects=True, vmem_limit_bytes=40 * 2**20
        ),
        cost_estimate=pl.CostEstimate(flops=4_600_000_000, bytes_accessed=5_300_000, transcendentals=0),
        name="sweep",
    )(*[
        pltpu.with_memory_space_constraint(array, pltpu.HBM)
        for array in (impedance[0, 0], rebuild_map[0, 0], left_trace[0, 0], lower_trace[0, 0], cell_kind, kind_wavenum)
    ])
    right, upper, residual = pl.pallas_call(
        flush,
        out_shape=[jax.ShapeDtypeStruct((rows, sources), bf16)] * 2 + [jax.ShapeDtypeStruct((cells, sources), f32)],
        in_specs=[pl.BlockSpec(memory_space=pltpu.VMEM)] * 3,
        out_specs=[pl.BlockSpec(memory_space=pl.ANY)] * 3,
        scratch_shapes=[pltpu.SemaphoreType.DMA((2 + chunks,))],
        name="flush",
    )(*[pltpu.with_memory_space_constraint(array, pltpu.VMEM) for array in (right, upper, residual)])
    return right[None, None], upper[None, None], residual.reshape(cx, cy, sources)


def solution(mesh):
    return jax.shard_map(
        functools.partial(per_device, mesh.shape["gx"], mesh.shape["gy"]),
        mesh=mesh,
        in_specs=(
            P("gx", "gy", None, None),
            P("gx", "gy", None, None),
            P("gx", "gy", None, None),
            P("gx", "gy", None, None),
            P("gx", "gy"),
            P(),
        ),
        out_specs=(P("gx", "gy", None, None), P("gx", "gy", None, None), P("gx", "gy", None)),
        check_vma=False,
    )
```

time: 61.5 us -> 55.7 us (0.906)
  the two profiles are of different devices: /device:TPU:11 before, /device:TPU:1 now
where the time goes in v2:
time: 55.7 us; the launch traced here: 55.6 us
  Pallas kernels  55 us (99%)
  between operations  0.64 us (1%)
    pallas_call x1, Pallas kernels, per_device(): pl.pallas_call(functools.partial(sweep, n_gx, n_gy), out_shape=(pltpu.VME...  53.8 us
    pallas_call x1, Pallas kernels, per_device(): pl.pallas_call(flush, out_shape=[jax.ShapeDtypeStruct((rows, sources), bf...  1.18 us

profile of v2, /device:TPU:1, one launch (start us, length us, event | category | flops | bytes accessed | tf_op | source)
XLA Modules:
  0.0 55.6 jit_solution(14902875840875624433)
XLA Ops:
  0.6 53.8 %sweep.1 = (bf16[512,512]{1,0:T(8,128)(2,1)S(1)}, bf16[512,512]{1,0:T(8,128)(2,1)S(1)}, f32[4,256,128]{2,1,0:T(8,128)S(1)}) custom-call(bf16[1024,1024]{1,0:T(8,128)(2,1)} %bitcast.7, bf16[256,1024]{1,0:T(8,128)(2,1)} %bitcast.8, bf16[512,512]{1,0:T(8,128)(2,1)} %bitcast.9, bf16[512,512]{1,0:T(8,128)(2,1)} %bitcast.10, s32[16,16]{1,0:T(8,128)} %kinds_hbm.1, ...), custom_call_target="tpu_custom_call" | custom-call | flops 4600000000 | bytes 5300000 | tf_op jit(solution)/shard_map/sweep/pallas_call | solution.py:342
  54.4 1.2 %flush.1 = (bf16[512,512]{1,0:T(8,128)(2,1)}, bf16[512,512]{1,0:T(8,128)(2,1)}, f32[256,512]{1,0:T(8,128)}) custom-call(bf16[512,512]{1,0:T(8,128)(2,1)S(1)} %get-tuple-element.9.right, bf16[512,512]{1,0:T(8,128)(2,1)S(1)} %get-tuple-element.10.upper, f32[4,256,128]{2,1,0:T(8,128)S(1)} %get-tuple-element.11.residual), custom_call_target="tpu_custom_call" | custom-call | tf_op jit(solution)/shard_map/flush/pallas_call | solution.py:380

commit v3 on v2

--- a/solution.py
+++ b/solution.py
@@ -23,7 +23,9 @@
     impedance, rebuild_map, left, lower, kinds_hbm, wavenum_hbm,
     right_out, upper_out, residual,
     amap, bmap, traces, outgoing, way, emap, factor, beside, edge_out, edge_in,
+    lent, composed, early_out, early_in, joined,
     cell_kind, kind_wavenum, load_sem, map_sem, right_send, right_recv, upper_send, upper_recv, way_send, way_recv, edge_send, edge_recv,
+    lend_send, lend_recv, early_send, early_recv,
 ):
     gx, gy = lax.axis_index("gx"), lax.axis_index("gy")
     rows = left.shape[0]
@@ -72,6 +74,8 @@
         (gy > 0, (gx, below)),
         (gx == last_x, (half - 1, gy)),
         (gx == half, (last_x, gy)),
+        ((gx == half) & (lax.rem(gy, 2) == 0) & (gy > 0), (0, below)),
+        ((gx == 0) & (lax.rem(gy, 2) == 0) & (gy > 0), (half, gy)),
     )
     for present, device in senders:
         @pl.when(present)
@@ -79,7 +83,11 @@
             pl.semaphore_signal(barrier, inc=1, device_id=device, device_id_type=MESH)
 
     greeted = 0
-    for present in (gx < last_x, gy < last_y, gx == half - 1, gx == last_x):
+    for present in (
+        gx < last_x, gy < last_y, gx == half - 1, gx == last_x,
+        (gx == 0) & (lax.rem(gy, 2) == 1) & (gy < last_y),
+        (gx == half) & (lax.rem(gy, 2) == 0) & (gy > 0),
+    ):
         greeted = greeted + jnp.where(present, 1, 0)
 
     def to_right(s, c):
@@ -105,7 +113,7 @@
         )
 
     def is_way(s, c):
-        return ((s == 0) & (c >= chunks // 2)) | ((s == 1) & (lax.rem(c, 2) == 0))
+        return ((s == 0) & (c >= chunks // 2))
 
     def send_right(s, c):
         by_way = (gx == half - 1) & is_way(s, c)
@@ -133,13 +141,37 @@
             to_way(s, c).wait_recv()
             from_way(s, c).start()
 
+    odd = lax.rem(gy, 2) == 1
+    detour = (gx == 0) & odd & (gy < last_y)
+    beside_me = (gx == half) & jnp.logical_not(odd) & (gy > 0)
+
+    def to_beside(s, c):
+        return remote(
+            outgoing.at[s, c, pl.ds(rows, rows), :], way.at[s, c], upper_send.at[s, c], way_recv.at[s, c], (half, above)
+        )
+
+    def from_beside(s, c):
+        return remote(
+            way.at[s, c], traces.at[s + 1, c, pl.ds(rows, rows), :], way_send.at[s, c], upper_recv.at[s, c], (0, gy)
+        )
+
+    def beside_relay(s, c):
+        @pl.when(beside_me)
+        def _():
+            to_beside(s, c).wait_recv()
+            from_beside(s, c).start()
+
     def multiply(s, c):
         return jnp.dot(amap[...], traces[s, c], preferred_element_type=jnp.float32).astype(jnp.bfloat16)
 
     def send_upper(s, c):
-        @pl.when(gy < last_y)
+        @pl.when((gy < last_y) & jnp.logical_not(detour))
         def _():
             to_upper(s, c).start()
+
+        @pl.when(detour)
+        def _():
+            to_beside(s, c).start()
 
     def advance(s, c):
         outgoing[s, c] = multiply(s, c)
@@ -165,6 +197,10 @@
         trace_load(1, c).wait()
         advance(0, c)
 
+    @pl.loop(0, chunks)
+    def _(c):
+        beside_relay(0, c)
+
     def clear(side):
         @pl.loop(1, STEPS)
         def _(s):
@@ -204,24 +240,77 @@
         jnp.where(chosen, 1.0, 0.0).astype(jnp.bfloat16), bmap[...], preferred_element_type=jnp.float32
     ).astype(jnp.bfloat16)
 
+    from_left, from_lower = gx == half - 2, (gx == half - 1) & (gy < last_y)
+    joins, joins_lower = gx == half - 1, (gx == half - 1) & (gy > 0)
+
+    def lend(k):
+        return remote(
+            bmap.at[pl.ds(cells - cy, cy), pl.ds(k * rows, rows)], lent.at[k], lend_send.at[k], lend_recv.at[k],
+            ((behind, gy), (gx, below))[k],
+        )
+
+    def early(k, c):
+        return remote(
+            early_out.at[c], early_in.at[k, c], early_send.at[c], early_recv.at[k, c], ((ahead, gy), (gx, above))[k]
+        )
+
+    def lend_rows():
+        for k, present in enumerate((joins, joins_lower)):
+            @pl.when(present)
+            def _(k=k):
+                lend(k).start()
+
+    def compose():
+        for k, present in enumerate((from_left, from_lower)):
+            @pl.when(present)
+            def _(k=k):
+                lend(k).wait_recv()
+                composed[...] = jnp.dot(
+                    lent[k], amap[pl.ds(k * rows, rows), :], preferred_element_type=jnp.float32
+                ).astype(composed.dtype)
+
+    def send_early(c):
+        @pl.when(from_left | from_lower)
+        def _():
+            early_out[c] = jnp.dot(
+                composed[...], traces[STEPS - 2, c], preferred_element_type=jnp.float32
+            ).astype(early_out.dtype)
+
+        for k, present in enumerate((from_left, from_lower)):
+            @pl.when(present)
+            def _(k=k):
+                early(k, c).start()
+
+    @pl.when((gx == half - 1) & (gy == 0))
+    def _():
+        early_in[1] = jnp.zeros(early_in.shape[1:], early_in.dtype)
+
     @pl.loop(1, STEPS - 1)
     def _(s):
         @pl.loop(0, chunks)
         def _(c):
             arrived(s - 1, c)
+
+            @pl.when((s == 1) & (c == 0))
+            def _():
+                lend_rows()
+
+            @pl.when((s == 2) & (c == 0))
+            def _():
+                compose()
+
+            @pl.when(s == 2)
+            def _():
+                send_early(c)
+
             advance(s, c)
 
             @pl.when((s == 1) & (c < chunks // 2))
             def _():
                 relay(0, c + chunks // 2)
 
-            @pl.when((s == 1) & (c == chunks // 2))
-            def _():
-                relay(1, 0)
-
-            @pl.when((s == 2) & (c == 0))
-            def _():
-                relay(1, chunks // 2)
+            beside_relay(s, c)
+
 
     reach = (
         (gx > 0, gx < last_x, (ahead, gy)),
@@ -230,6 +319,22 @@
         (gy < last_y, gy > 0, (gx, below)),
     )
 
+    def join_early():
+        @pl.when(joins)
+        def _():
+            @pl.loop(0, chunks)
+            def _(c):
+                early(0, c).wait_recv()
+
+                @pl.when(gy > 0)
+                def _():
+                    early(1, c).wait_recv()
+
+                joined[c] = (early_in[0, c].astype(jnp.float32) + early_in[1, c].astype(jnp.float32)).astype(joined.dtype)
+                remote(
+                    joined.at[c], edge_in.at[c, pl.ds(0, cy), :], edge_send.at[0, c], edge_recv.at[0, c], (ahead, gy)
+                ).start()
+
     def edge_copy(k, c):
         part = pl.ds(k * cy, cy)
         return remote(
@@ -241,7 +346,7 @@
             emap[...], traces[STEPS - 1, c], preferred_element_type=jnp.float32
         ).astype(edge_out.dtype)
         for k in range(4):
-            @pl.when(reach[k][1])
+            @pl.when(reach[k][1] & jnp.logical_not(joins) if k == 0 else reach[k][1])
             def _(k=k):
                 edge_copy(k, c).start()
 
@@ -272,6 +377,7 @@
 
         @pl.when(c == 0)
         def _():
+            join_early()
             kinds_load().wait()
             wavenum_load().wait()
 
@@ -288,11 +394,9 @@
         right_out[:, lanes] = leaving[:rows]
         upper_out[:, lanes] = leaving[rows:]
 
-        @pl.when(c > 0)
-        def _():
-            finish(c - 1)
-
-    finish(chunks - 1)
+    @pl.loop(0, chunks)
+    def _(c):
+        finish(c)
 
     @pl.loop(0, STEPS - 1)
     def _(s):
@@ -306,6 +410,10 @@
             def _():
                 from_way(s, c).wait_send()
 
+            @pl.when(beside_me)
+            def _():
+                from_beside(s, c).wait_send()
+
             @pl.when(gy < last_y)
             def _():
                 to_upper(s, c).wait_send()
@@ -316,6 +424,16 @@
             @pl.when(reach[k][1])
             def _(k=k):
                 edge_copy(k, c).wait_send()
+
+        for k, present in enumerate((from_left, from_lower)):
+            @pl.when(present)
+            def _(k=k):
+                early(k, c).wait_send()
+
+    for k, present in enumerate((joins, joins_lower)):
+        @pl.when(present)
+        def _(k=k):
+            lend(k).wait_send()
 
 
 def flush(right, upper, residual, right_out, upper_out, residual_out, sem):
@@ -359,6 +477,11 @@
             pltpu.VMEM((2, cells, LANES), f32),
             pltpu.VMEM((chunks, 4 * cy, LANES), bf16),
             pltpu.VMEM((chunks, 4 * cy, LANES), bf16),
+            pltpu.VMEM((2, cy, rows), bf16),
+            pltpu.VMEM((cy, 2 * rows), bf16),
+            pltpu.VMEM((chunks, cy, LANES), bf16),
+            pltpu.VMEM((2, chunks, cy, LANES), bf16),
+            pltpu.VMEM((chunks, cy, LANES), bf16),
             pltpu.SMEM((cx, cy), jnp.int32),
             pltpu.SMEM(kind_wavenum.shape, f32),
             pltpu.SemaphoreType.DMA((2, chunks)),
@@ -367,6 +490,9 @@
             *pair(STEPS - 1, chunks),
             *pair(STEPS - 1, chunks),
             *pair(4, chunks),
+            *pair(2),
+            pltpu.SemaphoreType.DMA((chunks,)),
+            pltpu.SemaphoreType.DMA((2, chunks)),
         ],
         compiler_params=pltpu.CompilerParams(
             collective_id=0, has_side_effects=True, vmem_limit_bytes=40 * 2**20

time: 55.7 us -> 52.9 us (0.950)
  Pallas kernels: 55 us -> 52.1 us
    pallas_call x1, Pallas kernels: 53.8 us -> 50.9 us  [per_device(): pl.pallas_call(functools.partial(sweep, n_gx, n_gy), out_shape=(pltpu.VME...]
where the time goes in v3:
time: 52.9 us; the launch traced here: 52.8 us
  Pallas kernels  52.1 us (98%)
  between operations  0.64 us (1%)
    pallas_call x1, Pallas kernels, per_device(): pl.pallas_call(functools.partial(sweep, n_gx, n_gy), out_shape=(pltpu.VME...  50.9 us
    pallas_call x1, Pallas kernels, per_device(): pl.pallas_call(flush, out_shape=[jax.ShapeDtypeStruct((rows, sources), bf...  1.18 us

profile of v3, /device:TPU:1, one launch (start us, length us, event | category | flops | bytes accessed | tf_op | source)
XLA Modules:
  0.0 52.8 jit_solution(4143450670176626185)
XLA Ops:
  0.6 50.9 %sweep.1 = (bf16[512,512]{1,0:T(8,128)(2,1)S(1)}, bf16[512,512]{1,0:T(8,128)(2,1)S(1)}, f32[4,256,128]{2,1,0:T(8,128)S(1)}) custom-call(bf16[1024,1024]{1,0:T(8,128)(2,1)} %bitcast.7, bf16[256,1024]{1,0:T(8,128)(2,1)} %bitcast.8, bf16[512,512]{1,0:T(8,128)(2,1)} %bitcast.9, bf16[512,512]{1,0:T(8,128)(2,1)} %bitcast.10, s32[16,16]{1,0:T(8,128)} %kinds_hbm.1, ...), custom_call_target="tpu_custom_call" | custom-call | flops 4600000000 | bytes 5300000 | tf_op jit(solution)/shard_map/sweep/pallas_call | solution.py:460
  51.6 1.2 %flush.1 = (bf16[512,512]{1,0:T(8,128)(2,1)}, bf16[512,512]{1,0:T(8,128)(2,1)}, f32[256,512]{1,0:T(8,128)}) custom-call(bf16[512,512]{1,0:T(8,128)(2,1)S(1)} %get-tuple-element.9.right, bf16[512,512]{1,0:T(8,128)(2,1)S(1)} %get-tuple-element.10.upper, f32[4,256,128]{2,1,0:T(8,128)S(1)} %get-tuple-element.11.residual), custom_call_target="tpu_custom_call" | custom-call | tf_op jit(solution)/shard_map/flush/pallas_call | solution.py:506

commit v4 on v3

--- a/solution.py
+++ b/solution.py
@@ -165,11 +165,11 @@
         return jnp.dot(amap[...], traces[s, c], preferred_element_type=jnp.float32).astype(jnp.bfloat16)
 
     def send_upper(s, c):
-        @pl.when((gy < last_y) & jnp.logical_not(detour))
+        @pl.when((gy < last_y) & jnp.logical_not(detour & (s > 0)))
         def _():
             to_upper(s, c).start()
 
-        @pl.when(detour)
+        @pl.when(detour & (s > 0))
         def _():
             to_beside(s, c).start()
 
@@ -197,10 +197,6 @@
         trace_load(1, c).wait()
         advance(0, c)
 
-    @pl.loop(0, chunks)
-    def _(c):
-        beside_relay(0, c)
-
     def clear(side):
         @pl.loop(1, STEPS)
         def _(s):
@@ -281,6 +277,18 @@
             def _(k=k):
                 early(k, c).start()
 
+    def join_early(c):
+        early(0, c).wait_recv()
+
+        @pl.when(gy > 0)
+        def _():
+            early(1, c).wait_recv()
+
+        joined[c] = (early_in[0, c].astype(jnp.float32) + early_in[1, c].astype(jnp.float32)).astype(joined.dtype)
+        remote(
+            joined.at[c], edge_in.at[c, pl.ds(0, cy), :], edge_send.at[0, c], edge_recv.at[0, c], (ahead, gy)
+        ).start()
+
     @pl.when((gx == half - 1) & (gy == 0))
     def _():
         early_in[1] = jnp.zeros(early_in.shape[1:], early_in.dtype)
@@ -310,6 +318,12 @@
                 relay(0, c + chunks // 2)
 
             beside_relay(s, c)
+
+            @pl.when(joins & (s == STEPS - 2) & (c == chunks - 1))
+            def _():
+                @pl.loop(0, chunks - 1)
+                def _(k):
+                    join_early(k)
 
 
     reach = (
@@ -318,22 +332,6 @@
         (gy > 0, gy < last_y, (gx, above)),
         (gy < last_y, gy > 0, (gx, below)),
     )
-
-    def join_early():
-        @pl.when(joins)
-        def _():
-            @pl.loop(0, chunks)
-            def _(c):
-                early(0, c).wait_recv()
-
-                @pl.when(gy > 0)
-                def _():
-                    early(1, c).wait_recv()
-
-                joined[c] = (early_in[0, c].astype(jnp.float32) + early_in[1, c].astype(jnp.float32)).astype(joined.dtype)
-                remote(
-                    joined.at[c], edge_in.at[c, pl.ds(0, cy), :], edge_send.at[0, c], edge_recv.at[0, c], (ahead, gy)
-                ).start()
 
     def edge_copy(k, c):
         part = pl.ds(k * cy, cy)
@@ -377,7 +375,10 @@
 
         @pl.when(c == 0)
         def _():
-            join_early()
+            @pl.when(joins)
+            def _():
+                join_early(chunks - 1)
+
             kinds_load().wait()
             wavenum_load().wait()
 
@@ -410,7 +411,7 @@
             def _():
                 from_way(s, c).wait_send()
 
-            @pl.when(beside_me)
+            @pl.when(beside_me & (s > 0))
             def _():
                 from_beside(s, c).wait_send()
 

time: 52.9 us -> 52.2 us (0.987)
  Pallas kernels: 52.1 us -> 51.4 us
    pallas_call x1, Pallas kernels: 50.9 us -> 50.2 us  [per_device(): pl.pallas_call(functools.partial(sweep, n_gx, n_gy), out_shape=(pltpu.VME...]
where the time goes in v4:
time: 52.2 us; the launch traced here: 52 us
  Pallas kernels  51.4 us (98%)
  between operations  0.64 us (1%)
    pallas_call x1, Pallas kernels, per_device(): pl.pallas_call(functools.partial(sweep, n_gx, n_gy), out_shape=(pltpu.VME...  50.2 us
    pallas_call x1, Pallas kernels, per_device(): pl.pallas_call(flush, out_shape=[jax.ShapeDtypeStruct((rows, sources), bf...  1.18 us

profile of v4, /device:TPU:1, one launch (start us, length us, event | category | flops | bytes accessed | tf_op | source)
XLA Modules:
  0.0 52.0 jit_solution(7069609504322832877)
XLA Ops:
  0.6 50.2 %sweep.1 = (bf16[512,512]{1,0:T(8,128)(2,1)S(1)}, bf16[512,512]{1,0:T(8,128)(2,1)S(1)}, f32[4,256,128]{2,1,0:T(8,128)S(1)}) custom-call(bf16[1024,1024]{1,0:T(8,128)(2,1)} %bitcast.7, bf16[256,1024]{1,0:T(8,128)(2,1)} %bitcast.8, bf16[512,512]{1,0:T(8,128)(2,1)} %bitcast.9, bf16[512,512]{1,0:T(8,128)(2,1)} %bitcast.10, s32[16,16]{1,0:T(8,128)} %kinds_hbm.1, ...), custom_call_target="tpu_custom_call" | custom-call | flops 4600000000 | bytes 5300000 | tf_op jit(solution)/shard_map/sweep/pallas_call | solution.py:461
  50.8 1.2 %flush.1 = (bf16[512,512]{1,0:T(8,128)(2,1)}, bf16[512,512]{1,0:T(8,128)(2,1)}, f32[256,512]{1,0:T(8,128)}) custom-call(bf16[512,512]{1,0:T(8,128)(2,1)S(1)} %get-tuple-element.9.right, bf16[512,512]{1,0:T(8,128)(2,1)S(1)} %get-tuple-element.10.upper, f32[4,256,128]{2,1,0:T(8,128)S(1)} %get-tuple-element.11.residual), custom_call_target="tpu_custom_call" | custom-call | tf_op jit(solution)/shard_map/flush/pallas_call | solution.py:507
